TPU v7x, 32 devices: a whole 2x2x4 slice. The times are simulated.
32 devices in a mesh: blocks: 32 (over z, y, x, core).
Axes of the slice: x: 2, y: 2, z: 4, core: 2. Of those that a mesh axis runs over, the one named last changes fastest.
Arguments:
- features: bfloat16 [192, 512, 128], P('blocks'), may hold values from -6 to 6
- cotangent: bfloat16 [192, 512, 128], P('blocks'), may hold values from -6 to 6
- weight_one: bfloat16 [27, 128, 128], replicated, may hold values from -0.109375 to 0.109375
- weight_two: bfloat16 [27, 128, 128], replicated, may hold values from -0.109375 to 0.109375
- occupancy: int32 [192, 512], P('blocks'), may hold values 0 or 1
- neighbours: int32 [192, 26], P('blocks'), may hold values from -1 to 191, as said below
Outputs:
- output: bfloat16 [192, 512, 128], P('blocks')
- grad_features: bfloat16 [192, 512, 128], P('blocks')
- grad_one: float32 [27, 128, 128], replicated
- grad_two: float32 [27, 128, 128], replicated
Inputs may be any that keep to these rules, and one draw needn't show every extreme that they name: `neighbours`: the blocks are positions of a grid with one plane of the first coordinate a device: the first coordinate of a block is its device index. The link is symmetric (block q is p's neighbour at offset o exactly when p is q's at minus o). A neighbour at an offset whose first component is -1, 0 or +1 lies on the device before, the same device or the device after, respectively. The blocks of one device are in row-major order of their second and third coordinates.
All inputs are finite; a program needn't handle non-finite values. No bound on the sum of `occupancy` on one device may be relied on, other than what follows from the above.
Results may differ from a plain program's by a relative error of at most 0.0049.
Values may be sent and summed in bfloat16 or wider, within the bound.
A program may use at most 64 MiB of HBM per device.

v0:
```python
import functools

import jax
import jax.numpy as jnp
from jax import lax
from jax.experimental import pallas as pl
from jax.experimental.pallas import tpu as pltpu
from jax.sharding import PartitionSpec as P

ROOT = 0.7978845608028654
CUBE = 0.044715
F32, BF16 = jnp.float32, jnp.bfloat16


def mm(left, right):
    return jnp.dot(left, right, preferred_element_type=F32)


def fill_columns(cols, own, prev, after, slots, count):
    z = lax.broadcasted_iota(jnp.int32, (10, 8, 128), 1)

    def one_block(blk, _):
        for p in range(10):
            dx = 0 if p == 0 else 2 if p == 9 else 1

            def rows(b, c, lo, hi):
                slot = slots[blk, dx * 9 + b * 3 + c]
                if dx == 0:
                    part = prev[slot, lo:hi]
                elif dx == 2:
                    part = after[slot, lo:hi]
                else:
                    part = own[slot, p - 1, lo:hi]
                return part.astype(F32)

            lines = [
                jnp.concatenate(
                    [rows(0, c, 48, 64)[8:], rows(1, c, 0, 64), rows(2, c, 0, 16)[:8]], axis=0
                ).reshape(10, 8, 128)
                for c in range(3)
            ]
            shifted = [
                pltpu.roll(jnp.where(z == 7, lines[0], lines[1]), 1, 1),
                lines[1],
                pltpu.roll(jnp.where(z == 0, lines[2], lines[1]), 7, 1),
            ]
            for b in range(3):
                for c in range(3):
                    at = (b * 3 + c) * 128
                    cols[p % 2, p // 2, blk, :, at : at + 128] = (
                        shifted[c][b : b + 8].reshape(64, 128).astype(BF16)
                    )
        return 0

    lax.fori_loop(0, count, one_block, 0)


def fill_weights(wide, weight, flip):
    for a in range(3):
        for t in range(9):
            o = a * 9 + t
            tap = weight[26 - o].T if flip else weight[o]
            for pair, half in ((0, 0), (1, 1)) if a == 1 else ((0, 1),) if a == 0 else ((1, 0),):
                wide[pair, t * 128 : t * 128 + 128, half * 128 : half * 128 + 128] = tap


def conv_step(cols, wide, q, count):
    rows = count * 64
    part = lambda par, at: cols[par, at].reshape(rows, 1152)
    both = mm(part(1, q), wide[0]) + mm(part(0, q + 1), wide[1])
    even = both[:, :128] + mm(part(0, q), wide[0, :, 128:])
    odd = both[:, 128:] + mm(part(1, q + 1), wide[1, :, :128])
    return even, odd


def pad_halo(dst, src, count):
    dst[:count] = src
    dst[count] = jnp.zeros((64, 128), BF16)


def front_kernel(
    count, slots, feat, cot, mask, prev_f, prev_c, next_f, next_c, w1, w2,
    act, gpre, g1, g2,
    own_f, own_c, pf, pc, nf, nc, cols_f, cols_c, wide1, wide2, act_t, gpre_t,
):
    own_f[:count] = feat[...] * mask[...]
    own_c[:count] = cot[...] * mask[...]
    own_f[count] = jnp.zeros((8, 64, 128), BF16)
    own_c[count] = jnp.zeros((8, 64, 128), BF16)
    for dst, src in ((pf, prev_f), (pc, prev_c), (nf, next_f), (nc, next_c)):
        pad_halo(dst, src[...], count)
    fill_weights(wide1, w1, False)
    fill_weights(wide2, w2, True)
    fill_columns(cols_f, own_f, pf, nf, slots, count)
    fill_columns(cols_c, own_c, pc, nc, slots, count)
    rows = count * 64

    def step(q, _):
        pres = conv_step(cols_f, wide1, q, count)
        grads = conv_step(cols_c, wide2, q, count)
        for par in range(2):
            gate = mask[:, 2 * q + par].reshape(rows, 128).astype(F32)
            x = pres[par] * gate
            t = jnp.tanh(ROOT * (x + CUBE * (x * x * x)))
            cdf = 0.5 * (1.0 + t)
            slope = cdf + x * (0.5 * (1.0 - t * t)) * (ROOT * (1.0 + (3.0 * CUBE) * (x * x)))
            a = (x * cdf * gate).astype(BF16)
            g = (grads[par] * gate * slope).astype(BF16)
            act[:, 2 * q + par] = a.reshape(count, 64, 128)
            gpre[:, 2 * q + par] = g.reshape(count, 64, 128)
            act_t[q, par * 128 : par * 128 + 128] = a.T
            gpre_t[q, par * 128 : par * 128 + 128] = g.T
        return 0

    lax.fori_loop(0, 4, step, 0)

    for b in range(3):
        for cols, left, out, flip in ((cols_f, gpre_t, g1, False), (cols_c, act_t, g2, True)):
            part = lambda par, at, q: cols[par, at + q, :, :, b * 384 : b * 384 + 384].reshape(rows, 384)
            total = lambda par, at, lo, hi: sum(
                mm(left[q, lo:hi], part(par, at, q)) for q in range(4)
            )
            r1 = total(1, 0, 0, 256)
            r2 = total(0, 1, 0, 256)
            sums = (
                total(0, 0, 0, 128) + r1[128:],
                r1[:128] + r2[128:],
                r2[:128] + total(1, 1, 128, 256),
            )
            for a in range(3):
                for c in range(3):
                    o = a * 9 + b * 3 + c
                    tile = sums[a][:, c * 128 : c * 128 + 128]
                    if flip:
                        out[26 - o] = tile
                    else:
                        out[o] = tile.T


def back_kernel(
    count, slots, act, gpre, mask, prev_f, prev_c, next_f, next_c, w1, w2,
    out, gfeat,
    own_f, own_c, pf, pc, nf, nc, cols_f, cols_c, wide1, wide2,
):
    own_f[:count] = act[...]
    own_c[:count] = gpre[...]
    own_f[count] = jnp.zeros((8, 64, 128), BF16)
    own_c[count] = jnp.zeros((8, 64, 128), BF16)
    for dst, src in ((pf, prev_f), (pc, prev_c), (nf, next_f), (nc, next_c)):
        pad_halo(dst, src[...], count)
    fill_weights(wide1, w1, True)
    fill_weights(wide2, w2, False)
    fill_columns(cols_f, own_f, pf, nf, slots, count)
    fill_columns(cols_c, own_c, pc, nc, slots, count)
    rows = count * 64

    def step(q, _):
        outs = conv_step(cols_f, wide2, q, count)
        grads = conv_step(cols_c, wide1, q, count)
        for par in range(2):
            gate = mask[:, 2 * q + par].reshape(rows, 128).astype(F32)
            out[:, 2 * q + par] = (outs[par] * gate).astype(BF16).reshape(count, 64, 128)
            gfeat[:, 2 * q + par] = (grads[par] * gate).astype(BF16).reshape(count, 64, 128)
        return 0

    lax.fori_loop(0, 4, step, 0)


def shards(features, cotangent, weight_one, weight_two, occupancy, neighbours):
    count = features.shape[0]
    shape = (count, 8, 64, 128)
    peers = lax.axis_size("blocks")
    me = lax.axis_index("blocks")
    ups = [(i, i + 1) for i in range(peers - 1)]
    downs = [(i + 1, i) for i in range(peers - 1)]
    mask = jnp.broadcast_to(occupancy.astype(BF16).reshape(count, 8, 64, 1), shape)
    feat = features.reshape(shape)
    cot = cotangent.reshape(shape)
    own = jnp.broadcast_to(me * count + jnp.arange(count, dtype=jnp.int32)[:, None], (count, 1))
    links = jnp.concatenate([neighbours[:, :13], own, neighbours[:, 13:]], axis=1)
    base = (me + jnp.arange(27, dtype=jnp.int32) // 9 - 1) * count
    slots = jnp.where(links >= 0, links - base[None], count).astype(jnp.int32)

    def swap(first, second, gate):
        lows = [first[:, 0], second[:, 0]]
        highs = [first[:, 7], second[:, 7]]
        if gate is not None:
            lows = [v * gate[:, 0] for v in lows]
            highs = [v * gate[:, 7] for v in highs]
        before = lax.ppermute(jnp.stack(highs), "blocks", ups)
        after = lax.ppermute(jnp.stack(lows), "blocks", downs)
        return before[0], before[1], after[0], after[1]

    smem = pl.BlockSpec(memory_space=pltpu.SMEM)
    vmem = pl.BlockSpec(memory_space=pltpu.VMEM)
    padded = [pltpu.VMEM((count + 1, 8, 64, 128), BF16)] * 2 + [
        pltpu.VMEM((count + 1, 64, 128), BF16)
    ] * 4
    cols = [pltpu.VMEM((2, 5, count, 64, 1152), BF16)] * 2
    wides = [pltpu.VMEM((2, 1152, 256), BF16)] * 2
    params = pltpu.CompilerParams(vmem_limit_bytes=58 * 1024 * 1024)
    field = jax.ShapeDtypeStruct(shape, BF16)
    grad = jax.ShapeDtypeStruct((27, 128, 128), F32)
    act, gpre, g1, g2 = pl.pallas_call(
        functools.partial(front_kernel, count),
        out_shape=(field, field, grad, grad),
        in_specs=[smem] + [vmem] * 9,
        out_specs=(vmem,) * 4,
        scratch_shapes=padded + cols + wides + [pltpu.VMEM((4, 256, count * 64), BF16)] * 2,
        compiler_params=params,
        cost_estimate=pl.CostEstimate(flops=11 * 10**9, bytes_accessed=10**7, transcendentals=400000),
        name="front",
    )(slots, feat, cot, mask, *swap(feat, cot, mask), weight_one, weight_two)
    grad_one, grad_two = lax.psum((g1, g2), "blocks")
    out, gfeat = pl.pallas_call(
        functools.partial(back_kernel, count),
        out_shape=(field, field),
        in_specs=[smem] + [vmem] * 9,
        out_specs=(vmem,) * 2,
        scratch_shapes=padded + cols + wides,
        compiler_params=params,
        cost_estimate=pl.CostEstimate(flops=6 * 10**9, bytes_accessed=10**7, transcendentals=0),
        name="back",
    )(slots, act, gpre, mask, *swap(act, gpre, None), weight_one, weight_two)
    return (
        out.reshape(features.shape),
        gfeat.reshape(features.shape),
        grad_one,
        grad_two,
    )


def solution(mesh):
    return jax.shard_map(
        shards,
        mesh=mesh,
        in_specs=(
            P("blocks", None, None),
            P("blocks", None, None),
            P(),
            P(),
            P("blocks", None),
            P("blocks", None),
        ),
        out_specs=(P("blocks", None, None), P("blocks", None, None), P(), P()),
        check_vma=False,
    )
```

profile of v0, /device:TPU:0, one launch (start us, length us, event | category | flops | bytes accessed | tf_op | source)
XLA Modules:
  0.0 202.2 jit_solution(5293700371726622868)
XLA Ops:
  7.2 0.0 all-reduce.3.cloned.1.call-start
  7.2 0.7 convert_element_type.3
  7.9 0.1 broadcast_in_dim.22
  8.0 1.2 fusion
  9.3 2.4 %collective-permute-start = (bf16[2,6,64,128]{3,2,1,0:T(8,128)(2,1)S(1)}, bf16[2,6,64,128]{3,2,1,0:T(8,128)(2,1)S(1)}, u32[]{:S(2)}, u32[]{:S(2)}) collective-permute-start(bf16[2,6,64,128]{3,2,1,0:T(8,128)(2,1)S(1)} %pad_maximum_fusion), channel_id=1, source_target_pairs={{0,1},{1,2},{2,3},{3,4},{4,5},{5,6},{6,7},{7,8},{8,9},{9,10},{10,1... | collective-permute-start | bytes 589832 | tf_op jit(solution)/shard_map/ppermute | solution.py:190
  11.7 1.3 collective-permute-start.1
  13.0 0.8 fusion.8
  13.9 0.7 subtract_select_fusion.slots
  14.5 0.0 collective-permute-done
  14.5 0.7 slice_bitcast_fusion.12
  15.2 1.9 collective-permute-done.1
  17.1 0.7 slice_bitcast_fusion.8
  17.8 1.3 broadcast_in_dim.23.mask
  19.2 25.5 %front.1 = (bf16[6,8,64,128]{3,2,1,0:T(8,128)(2,1)}, bf16[6,8,64,128]{3,2,1,0:T(8,128)(2,1)}, f32[27,128,128]{2,1,0:T(8,128)}, f32[27,128,128]{2,1,0:T(8,128)}) custom-call(s32[6,27]{1,0:T(8,128)} %subtract_select_fusion.slots, bf16[6,8,64,128]{3,2,1,0:T(8,128)(2,1)} %bitcast.57, bf16[6,8,64,128]{3,2,1,0:T(8,128)(2,1)} %bitcast.59, ...), custom_call_target="tpu_custom_call" | custom-call | flops 11000000512 | bytes 10000000 | tf_op jit(solution)/shard_map/front/pallas_call | solution.py:204
  44.7 0.0 all-reduce.3.cloned.1.call-update
  44.7 1.0 slice_bitcast_fusion.2
  45.7 1.0 slice_bitcast_fusion.3
  46.6 6.1 %collective-permute-start.2 = (bf16[2,6,64,128]{3,2,1,0:T(8,128)(2,1)S(1)}, bf16[2,6,64,128]{3,2,1,0:T(8,128)(2,1)S(1)}, u32[]{:S(2)}, u32[]{:S(2)}) collective-permute-start(bf16[2,6,64,128]{3,2,1,0:T(8,128)(2,1)S(1)} %pad_maximum_fusion.2), channel_id=1, source_target_pairs={{0,1},{1,2},{2,3},{3,4},{4,5},{5,6},{6,7},{7,8},{8,9},{9,10},{10,1... | collective-permute-start | bytes 589832 | tf_op jit(solution)/shard_map/ppermute | solution.py:190
  52.8 1.3 collective-permute-start.3
  54.1 0.0 collective-permute-done.2
  54.1 0.7 slice_bitcast_fusion.4
  54.7 1.3 collective-permute-done.3
  56.1 0.7 slice_bitcast_fusion
  56.8 14.7 %back.1 = (bf16[6,8,64,128]{3,2,1,0:T(8,128)(2,1)}, bf16[6,8,64,128]{3,2,1,0:T(8,128)(2,1)}) custom-call(s32[6,27]{1,0:T(8,128)} %subtract_select_fusion.slots, bf16[6,8,64,128]{3,2,1,0:T(8,128)(2,1)} %get-tuple-element.10.act, bf16[6,8,64,128]{3,2,1,0:T(8,128)(2,1)} %get-tuple-element.11.gpre, bf16[6,8,64,128]{3,2,1,0:T(8,128)(2,1)} %broadcast_in_dim.23.mask, ...), custom_call_target="tpu_custom_call" | custom-call | flops 6000000000 | bytes 10000000 | tf_op jit(solution)/shard_map/back/pallas_call | solution.py:215
  71.5 119.7 %all-reduce.3.cloned.1.call-done = (f32[27,128,128]{2,1,0:T(8,128)}, f32[27,128,128]{2,1,0:T(8,128)}) async-done(((f32[27,128,128]{2,1,0:T(8,128)}, f32[27,128,128]{2,1,0:T(8,128)}), (f32[27,128,128]{2,1,0:T(8,128)}, f32[27,128,128]{2,1,0:T(8,128)})) %all-reduce.3.cloned.1.call-update) | async-done | bytes 3538960 | tf_op jit(solution)/shard_map/psum | solution.py:214
  191.1 0.0 copy-start
  191.1 3.0 %copy.47 = f32[27,128,128]{2,1,0:T(8,128)} copy(f32[27,128,128]{2,1,0:T(8,128)} %get-tuple-element.44) | data formatting | bytes 3538944
  194.2 0.0 copy-done
  194.2 1.2 copy.48
  (8 shorter events, 0.1 us)
Async XLA Ops:
  7.2 184.0 %all-reduce.3.cloned.1.call-start = ((), (), s32[]{:S(2)}) async-start(), calls=%async_computation | async-start | bytes 7077888 | tf_op jit(solution)/shard_map/psum | solution.py:214
  9.3 5.2 %collective-permute-start = (bf16[2,6,64,128]{3,2,1,0:T(8,128)(2,1)S(1)}, bf16[2,6,64,128]{3,2,1,0:T(8,128)(2,1)S(1)}, u32[]{:S(2)}, u32[]{:S(2)}) collective-permute-start(bf16[2,6,64,128]{3,2,1,0:T(8,128)(2,1)S(1)} %pad_maximum_fusion), channel_id=1, source_target_pairs={{0,1},{1,2},{2,3},{3,4},{4,5},{5,6},{6,7},{7,8},{8,9},{9,10},{10,1... | collective-permute-start | bytes 589832 | tf_op jit(solution)/shard_map/ppermute | solution.py:190
  11.7 5.4 %collective-permute-start.1 = (bf16[2,6,64,128]{3,2,1,0:T(8,128)(2,1)S(1)}, bf16[2,6,64,128]{3,2,1,0:T(8,128)(2,1)S(1)}, u32[]{:S(2)}, u32[]{:S(2)}) collective-permute-start(bf16[2,6,64,128]{3,2,1,0:T(8,128)(2,1)S(1)} %pad_maximum_fusion.1), channel_id=1, source_target_pairs={{1,0},{2,1},{3,2},{4,3},{5,4},{6,5},{7,6},{8,7},{9,8},{10,9},{11,1... | collective-permute-start | bytes 589832 | tf_op jit(solution)/shard_map/ppermute | solution.py:191
  46.6 7.4 %collective-permute-start.2 = (bf16[2,6,64,128]{3,2,1,0:T(8,128)(2,1)S(1)}, bf16[2,6,64,128]{3,2,1,0:T(8,128)(2,1)S(1)}, u32[]{:S(2)}, u32[]{:S(2)}) collective-permute-start(bf16[2,6,64,128]{3,2,1,0:T(8,128)(2,1)S(1)} %pad_maximum_fusion.2), channel_id=1, source_target_pairs={{0,1},{1,2},{2,3},{3,4},{4,5},{5,6},{6,7},{7,8},{8,9},{9,10},{10,1... | collective-permute-start | bytes 589832 | tf_op jit(solution)/shard_map/ppermute | solution.py:190
  52.8 3.3 %collective-permute-start.3 = (bf16[2,6,64,128]{3,2,1,0:T(8,128)(2,1)S(1)}, bf16[2,6,64,128]{3,2,1,0:T(8,128)(2,1)S(1)}, u32[]{:S(2)}, u32[]{:S(2)}) collective-permute-start(bf16[2,6,64,128]{3,2,1,0:T(8,128)(2,1)S(1)} %pad_maximum_fusion.3), channel_id=1, source_target_pairs={{1,0},{2,1},{3,2},{4,3},{5,4},{6,5},{7,6},{8,7},{9,8},{10,9},{11,1... | collective-permute-start | bytes 589832 | tf_op jit(solution)/shard_map/ppermute | solution.py:191
  191.1 3.0 %copy-start = (f32[27,128,128]{2,1,0:T(8,128)S(1)}, f32[27,128,128]{2,1,0:T(8,128)}, u32[]{:S(2)}) copy-start(f32[27,128,128]{2,1,0:T(8,128)} %get-tuple-element.45) | copy-start | bytes 5308420
Sparse Core Ops, SparseCore 0:
  44.8 146.2 all-reduce.2
where the time goes:
time: 203 us; the launch traced here: 202 us
  waiting for transfers between devices  123 us (61%)
  Pallas kernels  40.2 us (20%)
  between operations  14.1 us (7%)
  local copies, waits for them, and re-layouts  11.2 us (6%)
  starting transfers between devices  11.1 us (5%)
  other arithmetic  2.71 us (1%)
    psum x1, waiting for transfers between devices, shards(): grad_one, grad_two = lax.psum((g1, g2), 'blocks')  120 us
    pallas_call x1, Pallas kernels, shards(): pl.pallas_call(functools.partial(front_kernel, count), out_shape=(field,...  25.5 us
    pallas_call x1, Pallas kernels, shards(): pl.pallas_call(functools.partial(back_kernel, count), out_shape=(field, f...  14.7 us
    ppermute x2, starting transfers between devices, swap(): before = lax.ppermute(jnp.stack(highs), 'blocks', ups)  8.43 us
    unnamed x5, local copies, waits for them, and re-layouts  4.22 us
  transfers between devices with their start and end apart: 5, of which 3 were waited for; matrix products, arithmetic and copies ran while one was open for 3% of the time, Pallas kernels for 7%

commit v1 on v0

--- a/solution.py
+++ b/solution.py
@@ -80,7 +80,7 @@
 
 def front_kernel(
     count, slots, feat, cot, mask, prev_f, prev_c, next_f, next_c, w1, w2,
-    act, gpre, g1, g2,
+    act, gpre, grads_out,
     own_f, own_c, pf, pc, nf, nc, cols_f, cols_c, wide1, wide2, act_t, gpre_t,
 ):
     own_f[:count] = feat[...] * mask[...]
@@ -115,7 +115,7 @@
     lax.fori_loop(0, 4, step, 0)
 
     for b in range(3):
-        for cols, left, out, flip in ((cols_f, gpre_t, g1, False), (cols_c, act_t, g2, True)):
+        for cols, left, flip in ((cols_f, gpre_t, False), (cols_c, act_t, True)):
             part = lambda par, at, q: cols[par, at + q, :, :, b * 384 : b * 384 + 384].reshape(rows, 384)
             total = lambda par, at, lo, hi: sum(
                 mm(left[q, lo:hi], part(par, at, q)) for q in range(4)
@@ -131,10 +131,111 @@
                 for c in range(3):
                     o = a * 9 + b * 3 + c
                     tile = sums[a][:, c * 128 : c * 128 + 128]
-                    if flip:
-                        out[26 - o] = tile
-                    else:
-                        out[o] = tile.T
+                    tap = 53 - o if flip else o
+                    at = tap % 18 * 128
+                    grads_out[tap // 18, at : at + 128] = tile if flip else tile.T
+    for part in range(3):
+        spare = grads_out.shape[1] - 2304
+        grads_out[part, 2304:] = jnp.zeros((spare, 128), F32)
+
+
+def sum_steps(peers, grads, total, outbox, inbox, result, sems):
+    me = lax.axis_index("blocks")
+    bits = peers.bit_length() - 1
+    send, recv, send_all, recv_all = sems
+    orders, lows, signs = [], [], []
+    for part in range(3):
+        turn = part * (bits - 1) // 3
+        rest = list(range(1, bits))
+        order = [0] + rest[turn:] + rest[:turn]
+        low, lo, sign = 0, [0], []
+        for s, k in enumerate(order):
+            bit = me // 2**k % 2
+            low = low + bit * (peers >> (s + 1))
+            lo.append(low)
+            sign.append(bit)
+        orders.append(order)
+        lows.append(lo)
+        signs.append(sign)
+
+    def partner(part, s):
+        return me + 2 ** orders[part][s] * (1 - 2 * signs[part][s])
+
+    def halve(part, s):
+        half = peers >> (s + 1)
+        other = lows[part][s] + (1 - signs[part][s]) * half
+        at = peers - (peers >> s)
+        return other, half, at, pltpu.make_async_remote_copy(
+            src_ref=outbox.at[part, pl.ds(other, half)],
+            dst_ref=inbox.at[part, pl.ds(at, half)],
+            send_sem=send.at[part, s],
+            recv_sem=recv.at[part, s],
+            device_id=(partner(part, s),),
+            device_id_type=pl.DeviceIdType.MESH,
+        )
+
+    def double(part, s):
+        held = pl.ds(lows[part][s + 1], peers >> (s + 1))
+        return pltpu.make_async_remote_copy(
+            src_ref=result.at[part, held],
+            dst_ref=result.at[part, held],
+            send_sem=send_all.at[part, s],
+            recv_sem=recv_all.at[part, s],
+            device_id=(partner(part, s),),
+            device_id_type=pl.DeviceIdType.MESH,
+        )
+
+    def start_halve(s):
+        source = grads if s == 0 else total
+        for part in range(3):
+            other, half, _, copy = halve(part, s)
+            outbox[part, pl.ds(other, half)] = source[part, pl.ds(other, half)].astype(BF16)
+            copy.start()
+
+    def finish_halve(s):
+        source = grads if s == 0 else total
+        for part in range(3):
+            _, half, at, copy = halve(part, s)
+            copy.wait()
+            mine = pl.ds(lows[part][s + 1], half)
+            value = source[part, mine] + inbox[part, at : at + half].astype(F32)
+            if s == bits - 1:
+                result[part, mine] = value.astype(BF16)
+            else:
+                total[part, mine] = value
+
+    def start_double(s):
+        for part in range(3):
+            double(part, s).start()
+
+    def finish_double(s):
+        for part in range(3):
+            double(part, s).wait()
+
+    steps = [(functools.partial(start_halve, s), functools.partial(finish_halve, s)) for s in range(bits)]
+    steps += [
+        (functools.partial(start_double, s), functools.partial(finish_double, s))
+        for s in reversed(range(bits))
+    ]
+    return steps
+
+
+def greet(peers):
+    me = lax.axis_index("blocks")
+    bits = peers.bit_length() - 1
+    barrier = pltpu.get_barrier_semaphore()
+    for k in range(bits):
+        other = me + 2**k * (1 - 2 * (me // 2**k % 2))
+        pl.semaphore_signal(barrier, inc=1, device_id=(other,), device_id_type=pl.DeviceIdType.MESH)
+    pl.semaphore_wait(barrier, bits)
+
+
+def sum_kernel(peers, grads, summed, total, outbox, inbox, result, *sems):
+    greet(peers)
+    for start, finish in sum_steps(peers, grads, total, outbox, inbox, result, sems):
+        start()
+        finish()
+    summed[...] = result[...]
 
 
 def back_kernel(
@@ -200,18 +301,35 @@
     wides = [pltpu.VMEM((2, 1152, 256), BF16)] * 2
     params = pltpu.CompilerParams(vmem_limit_bytes=58 * 1024 * 1024)
     field = jax.ShapeDtypeStruct(shape, BF16)
-    grad = jax.ShapeDtypeStruct((27, 128, 128), F32)
-    act, gpre, g1, g2 = pl.pallas_call(
+    chunk = -(-2304 // (16 * peers)) * 16
+    bits = peers.bit_length() - 1
+    grad = jax.ShapeDtypeStruct((3, chunk * peers, 128), F32)
+    act, gpre, grads = pl.pallas_call(
         functools.partial(front_kernel, count),
-        out_shape=(field, field, grad, grad),
+        out_shape=(field, field, grad),
         in_specs=[smem] + [vmem] * 9,
-        out_specs=(vmem,) * 4,
+        out_specs=(vmem,) * 3,
         scratch_shapes=padded + cols + wides + [pltpu.VMEM((4, 256, count * 64), BF16)] * 2,
         compiler_params=params,
         cost_estimate=pl.CostEstimate(flops=11 * 10**9, bytes_accessed=10**7, transcendentals=400000),
         name="front",
     )(slots, feat, cot, mask, *swap(feat, cot, mask), weight_one, weight_two)
-    grad_one, grad_two = lax.psum((g1, g2), "blocks")
+    pieces = (3, peers, chunk, 128)
+    bridge = [pltpu.VMEM(pieces, F32)] + [pltpu.VMEM(pieces, BF16)] * 3
+    bridge += [pltpu.SemaphoreType.DMA((3, bits))] * 4
+    summed = pl.pallas_call(
+        functools.partial(sum_kernel, peers),
+        out_shape=jax.ShapeDtypeStruct(pieces, BF16),
+        in_specs=[vmem],
+        out_specs=vmem,
+        scratch_shapes=bridge,
+        compiler_params=pltpu.CompilerParams(
+            vmem_limit_bytes=58 * 1024 * 1024, collective_id=0, has_side_effects=True
+        ),
+        name="total",
+    )(grads.reshape(pieces))
+    summed = summed.reshape(3, chunk * peers, 128)[:, :2304].reshape(54, 128, 128).astype(F32)
+    grad_one, grad_two = summed[:27], summed[27:]
     out, gfeat = pl.pallas_call(
         functools.partial(back_kernel, count),
         out_shape=(field, field),

time: 203 us -> 122 us (0.60)
  the two profiles are of different devices: /device:TPU:0 before, /device:TPU:7 now
where the time goes in v1:
time: 122 us; the launch traced here: 121 us
  Pallas kernels  86.1 us (71%)
  starting transfers between devices  12.3 us (10%)
  local copies, waits for them, and re-layouts  10.8 us (9%)
  waiting for transfers between devices  8.4 us (7%)
  other arithmetic  2.71 us (2%)
    pallas_call x1, Pallas kernels, shards(): pl.pallas_call(functools.partial(sum_kernel, peers), out_shape=jax.ShapeD...  45.8 us
    pallas_call x1, Pallas kernels, shards(): pl.pallas_call(functools.partial(front_kernel, count), out_shape=(field,...  25.6 us
    pallas_call x1, Pallas kernels, shards(): pl.pallas_call(functools.partial(back_kernel, count), out_shape=(field, f...  14.7 us
    ppermute x2, waiting for transfers between devices, swap(): after = lax.ppermute(jnp.stack(lows), 'blocks', downs)  8.4 us
    ppermute x2, starting transfers between devices, swap(): before = lax.ppermute(jnp.stack(highs), 'blocks', ups)  8.28 us
    ppermute x2, starting transfers between devices, swap(): after = lax.ppermute(jnp.stack(lows), 'blocks', downs)  4.02 us
    squeeze x4, local copies, waits for them, and re-layouts, swap(): return (before[0], before[1], after[0], after[1])  2.77 us
  transfers between devices with their start and end apart: 4, of which 2 were waited for; matrix products, arithmetic and copies ran while one was open for 4% of the time, Pallas kernels for 0%

profile of v1, /device:TPU:7, one launch (start us, length us, event | category | flops | bytes accessed | tf_op | source)
XLA Modules:
  0.0 121.1 jit_solution(15132075827981317082)
XLA Ops:
  0.6 0.7 convert_element_type.9
  1.4 0.1 broadcast_in_dim.22
  1.5 1.2 %fusion = (bf16[1,6,64,128]{3,2,1,0:T(8,128)(2,1)S(1)}, bf16[1,6,64,128]{3,2,1,0:T(8,128)(2,1)S(1)}, bf16[1,6,64,128]{3,2,1,0:T(8,128)(2,1)S(1)}, bf16[1,6,64,128]{3,2,1,0:T(8,128)(2,1)S(1)}) fusion(bf16[6,8,64,128]{3,2,1,0:T(8,128)(2,1)} %bitcast.65, bf16[6,64]{1,0:T(8,128)(2,1)S(1)} %get-tuple-element.38, bf16[6,64]{1,0:T(8,128)(2,1)S(1)} %get-tuple-element.39, ...), kind=kLoop, calls=%fused_computation.15 | loop fusion | flops 196608 | bytes 787968 | tf_op jit(solution)/shard_map/mul | solution.py:289
  2.7 3.7 %collective-permute-start = (bf16[2,6,64,128]{3,2,1,0:T(8,128)(2,1)S(1)}, bf16[2,6,64,128]{3,2,1,0:T(8,128)(2,1)S(1)}, u32[]{:S(2)}, u32[]{:S(2)}) collective-permute-start(bf16[2,6,64,128]{3,2,1,0:T(8,128)(2,1)S(1)} %pad_maximum_fusion), channel_id=1, source_target_pairs={{0,1},{1,2},{2,3},{3,4},{4,5},{5,6},{6,7},{7,8},{8,9},{9,10},{10,1... | collective-permute-start | bytes 589832 | tf_op jit(solution)/shard_map/ppermute | solution.py:291
  6.4 1.9 %collective-permute-start.1 = (bf16[2,6,64,128]{3,2,1,0:T(8,128)(2,1)S(1)}, bf16[2,6,64,128]{3,2,1,0:T(8,128)(2,1)S(1)}, u32[]{:S(2)}, u32[]{:S(2)}) collective-permute-start(bf16[2,6,64,128]{3,2,1,0:T(8,128)(2,1)S(1)} %pad_maximum_fusion.1), channel_id=1, source_target_pairs={{1,0},{2,1},{3,2},{4,3},{5,4},{6,5},{7,6},{8,7},{9,8},{10,9},{11,1... | collective-permute-start | bytes 589832 | tf_op jit(solution)/shard_map/ppermute | solution.py:292
  8.4 0.8 fusion.9
  9.2 0.7 subtract_select_fusion.slots
  9.9 0.0 collective-permute-done
  9.9 0.7 slice_bitcast_fusion.12
  10.6 4.6 %collective-permute-done.1 = bf16[2,6,64,128]{3,2,1,0:T(8,128)(2,1)S(1)} collective-permute-done((bf16[2,6,64,128]{3,2,1,0:T(8,128)(2,1)S(1)}, bf16[2,6,64,128]{3,2,1,0:T(8,128)(2,1)S(1)}, u32[]{:S(2)}, u32[]{:S(2)}) %collective-permute-start.1) | collective-permute-done | bytes 196640 | tf_op jit(solution)/shard_map/ppermute | solution.py:292
  15.2 0.7 slice_bitcast_fusion.8
  15.9 1.4 %broadcast_in_dim.23.mask = bf16[6,8,64,128]{3,2,1,0:T(8,128)(2,1)} broadcast(bf16[6,8,64]{2,1,0:T(8,128)(2,1)S(1)} %broadcast_in_dim.22), dimensions={0,1,2} | broadcast | bytes 792576 | tf_op jit(solution)/shard_map/broadcast_in_dim | solution.py:277
  17.3 25.6 %front.1 = (bf16[6,8,64,128]{3,2,1,0:T(8,128)(2,1)}, bf16[6,8,64,128]{3,2,1,0:T(8,128)(2,1)}, f32[3,2560,128]{2,1,0:T(8,128)}) custom-call(s32[6,27]{1,0:T(8,128)} %subtract_select_fusion.slots, bf16[6,8,64,128]{3,2,1,0:T(8,128)(2,1)} %bitcast.64, bf16[6,8,64,128]{3,2,1,0:T(8,128)(2,1)} %bitcast.66, bf16[6,8,64,128]{3,2,1,0:T(8,128)(2,1)} %broadcast_in_dim.23.mask, ...), custom_call_target="tpu_custom_call" | custom-call | flops 11000000512 | bytes 10000000 | tf_op jit(solution)/shard_map/front/pallas_call | solution.py:307
  42.9 45.8 %total.1 = bf16[3,32,80,128]{3,2,1,0:T(8,128)(2,1)} custom-call(f32[3,32,80,128]{3,2,1,0:T(8,128)} %bitcast.62), custom_call_target="tpu_custom_call" | custom-call | tf_op jit(solution)/shard_map/total/pallas_call | solution.py:320
  88.7 1.6 %slice.114 = bf16[3,2304,128]{2,1,0:T(8,128)(2,1)S(1)} slice(bf16[3,2560,128]{2,1,0:T(8,128)(2,1)} %bitcast.61), slice={[0:3], [0:2304], [0:128]} | slice | bytes 3538944 | tf_op jit(solution)/shard_map/slice | solution.py:331
  90.3 1.0 slice_bitcast_fusion.3
  91.3 1.0 slice_bitcast_fusion.2
  92.3 4.6 %collective-permute-start.2 = (bf16[2,6,64,128]{3,2,1,0:T(8,128)(2,1)S(1)}, bf16[2,6,64,128]{3,2,1,0:T(8,128)(2,1)S(1)}, u32[]{:S(2)}, u32[]{:S(2)}) collective-permute-start(bf16[2,6,64,128]{3,2,1,0:T(8,128)(2,1)S(1)} %pad_maximum_fusion.2), channel_id=1, source_target_pairs={{0,1},{1,2},{2,3},{3,4},{4,5},{5,6},{6,7},{7,8},{8,9},{9,10},{10,1... | collective-permute-start | bytes 589832 | tf_op jit(solution)/shard_map/ppermute | solution.py:291
  96.9 2.1 %collective-permute-start.3 = (bf16[2,6,64,128]{3,2,1,0:T(8,128)(2,1)S(1)}, bf16[2,6,64,128]{3,2,1,0:T(8,128)(2,1)S(1)}, u32[]{:S(2)}, u32[]{:S(2)}) collective-permute-start(bf16[2,6,64,128]{3,2,1,0:T(8,128)(2,1)S(1)} %pad_maximum_fusion.3), channel_id=1, source_target_pairs={{1,0},{2,1},{3,2},{4,3},{5,4},{6,5},{7,6},{8,7},{9,8},{10,9},{11,1... | collective-permute-start | bytes 589832 | tf_op jit(solution)/shard_map/ppermute | solution.py:292
  99.0 2.2 %fusion.7 = (f32[27,128,128]{2,1,0:T(8,128)}, f32[27,128,128]{2,1,0:T(8,128)}) fusion(bf16[54,128,128]{2,1,0:T(8,128)(2,1)S(1)} %bitcast.60), kind=kLoop, calls=%fused_computation.36 | loop fusion | bytes 7077888 | tf_op jit(solution)/shard_map/slice | solution.py:332
  101.3 0.0 collective-permute-done.2
  101.3 0.7 slice_bitcast_fusion.4
  101.9 3.8 %collective-permute-done.3 = bf16[2,6,64,128]{3,2,1,0:T(8,128)(2,1)S(1)} collective-permute-done((bf16[2,6,64,128]{3,2,1,0:T(8,128)(2,1)S(1)}, bf16[2,6,64,128]{3,2,1,0:T(8,128)(2,1)S(1)}, u32[]{:S(2)}, u32[]{:S(2)}) %collective-permute-start.3) | collective-permute-done | bytes 196640 | tf_op jit(solution)/shard_map/ppermute | solution.py:292
  105.7 0.7 slice_bitcast_fusion
  106.4 14.7 %back.1 = (bf16[6,8,64,128]{3,2,1,0:T(8,128)(2,1)}, bf16[6,8,64,128]{3,2,1,0:T(8,128)(2,1)}) custom-call(s32[6,27]{1,0:T(8,128)} %subtract_select_fusion.slots, bf16[6,8,64,128]{3,2,1,0:T(8,128)(2,1)} %get-tuple-element.9.act, bf16[6,8,64,128]{3,2,1,0:T(8,128)(2,1)} %get-tuple-element.10.gpre, bf16[6,8,64,128]{3,2,1,0:T(8,128)(2,1)} %broadcast_in_dim.23.mask, ...), custom_call_target="tpu_custom_call" | custom-call | flops 6000000000 | bytes 10000000 | tf_op jit(solution)/shard_map/back/pallas_call | solution.py:333
  (8 shorter events, 0.1 us)
Async XLA Ops:
  2.7 7.2 %collective-permute-start = (bf16[2,6,64,128]{3,2,1,0:T(8,128)(2,1)S(1)}, bf16[2,6,64,128]{3,2,1,0:T(8,128)(2,1)S(1)}, u32[]{:S(2)}, u32[]{:S(2)}) collective-permute-start(bf16[2,6,64,128]{3,2,1,0:T(8,128)(2,1)S(1)} %pad_maximum_fusion), channel_id=1, source_target_pairs={{0,1},{1,2},{2,3},{3,4},{4,5},{5,6},{6,7},{7,8},{8,9},{9,10},{10,1... | collective-permute-start | bytes 589832 | tf_op jit(solution)/shard_map/ppermute | solution.py:291
  6.4 8.8 %collective-permute-start.1 = (bf16[2,6,64,128]{3,2,1,0:T(8,128)(2,1)S(1)}, bf16[2,6,64,128]{3,2,1,0:T(8,128)(2,1)S(1)}, u32[]{:S(2)}, u32[]{:S(2)}) collective-permute-start(bf16[2,6,64,128]{3,2,1,0:T(8,128)(2,1)S(1)} %pad_maximum_fusion.1), channel_id=1, source_target_pairs={{1,0},{2,1},{3,2},{4,3},{5,4},{6,5},{7,6},{8,7},{9,8},{10,9},{11,1... | collective-permute-start | bytes 589832 | tf_op jit(solution)/shard_map/ppermute | solution.py:292
  92.3 9.0 %collective-permute-start.2 = (bf16[2,6,64,128]{3,2,1,0:T(8,128)(2,1)S(1)}, bf16[2,6,64,128]{3,2,1,0:T(8,128)(2,1)S(1)}, u32[]{:S(2)}, u32[]{:S(2)}) collective-permute-start(bf16[2,6,64,128]{3,2,1,0:T(8,128)(2,1)S(1)} %pad_maximum_fusion.2), channel_id=1, source_target_pairs={{0,1},{1,2},{2,3},{3,4},{4,5},{5,6},{6,7},{7,8},{8,9},{9,10},{10,1... | collective-permute-start | bytes 589832 | tf_op jit(solution)/shard_map/ppermute | solution.py:291
  96.9 8.8 %collective-permute-start.3 = (bf16[2,6,64,128]{3,2,1,0:T(8,128)(2,1)S(1)}, bf16[2,6,64,128]{3,2,1,0:T(8,128)(2,1)S(1)}, u32[]{:S(2)}, u32[]{:S(2)}) collective-permute-start(bf16[2,6,64,128]{3,2,1,0:T(8,128)(2,1)S(1)} %pad_maximum_fusion.3), channel_id=1, source_target_pairs={{1,0},{2,1},{3,2},{4,3},{5,4},{6,5},{7,6},{8,7},{9,8},{10,9},{11,1... | collective-permute-start | bytes 589832 | tf_op jit(solution)/shard_map/ppermute | solution.py:292

commit v2 on v1

--- a/solution.py
+++ b/solution.py
@@ -227,33 +227,55 @@
     for k in range(bits):
         other = me + 2**k * (1 - 2 * (me // 2**k % 2))
         pl.semaphore_signal(barrier, inc=1, device_id=(other,), device_id_type=pl.DeviceIdType.MESH)
-    pl.semaphore_wait(barrier, bits)
-
-
-def sum_kernel(peers, grads, summed, total, outbox, inbox, result, *sems):
+    for other in ((me + 1) % peers, (me + peers - 1) % peers):
+        pl.semaphore_signal(barrier, inc=1, device_id=(other,), device_id_type=pl.DeviceIdType.MESH)
+    pl.semaphore_wait(barrier, bits + 2)
+
+
+def back_kernel(
+    peers, count, slots, act, gpre, mask, w1, w2, grads,
+    out, gfeat, summed,
+    own_f, own_c, edges, halo, cols_f, cols_c, wide1, wide2,
+    total, outbox, inbox, result, edge_send, edge_recv, *sems,
+):
     greet(peers)
-    for start, finish in sum_steps(peers, grads, total, outbox, inbox, result, sems):
-        start()
-        finish()
-    summed[...] = result[...]
-
-
-def back_kernel(
-    count, slots, act, gpre, mask, prev_f, prev_c, next_f, next_c, w1, w2,
-    out, gfeat,
-    own_f, own_c, pf, pc, nf, nc, cols_f, cols_c, wide1, wide2,
-):
-    own_f[:count] = act[...]
-    own_c[:count] = gpre[...]
-    own_f[count] = jnp.zeros((8, 64, 128), BF16)
-    own_c[count] = jnp.zeros((8, 64, 128), BF16)
-    for dst, src in ((pf, prev_f), (pc, prev_c), (nf, next_f), (nc, next_c)):
-        pad_halo(dst, src[...], count)
-    fill_weights(wide1, w1, True)
-    fill_weights(wide2, w2, False)
-    fill_columns(cols_f, own_f, pf, nf, slots, count)
-    fill_columns(cols_c, own_c, pc, nc, slots, count)
+    me = lax.axis_index("blocks")
     rows = count * 64
+    steps = sum_steps(peers, grads, total, outbox, inbox, result, sems)
+    steps[0][0]()
+
+    for i, (field, x) in enumerate(((act, 7), (gpre, 7), (act, 0), (gpre, 0))):
+        edges[i, :count] = field[:, x]
+        edges[i, count] = jnp.zeros((64, 128), BF16)
+    swaps = []
+    for i, other in enumerate(((me + 1) % peers, (me + peers - 1) % peers)):
+        swaps.append(
+            pltpu.make_async_remote_copy(
+                src_ref=edges.at[pl.ds(2 * i, 2)],
+                dst_ref=halo.at[pl.ds(2 * i, 2)],
+                send_sem=edge_send.at[i],
+                recv_sem=edge_recv.at[i],
+                device_id=(other,),
+                device_id_type=pl.DeviceIdType.MESH,
+            )
+        )
+        swaps[i].start()
+
+    def weights():
+        own_f[:count] = act[...]
+        own_c[:count] = gpre[...]
+        own_f[count] = jnp.zeros((8, 64, 128), BF16)
+        own_c[count] = jnp.zeros((8, 64, 128), BF16)
+        fill_weights(wide1, w1, True)
+        fill_weights(wide2, w2, False)
+
+    def first_field():
+        for swap in swaps:
+            swap.wait()
+        fill_columns(cols_f, own_f, halo.at[0], halo.at[2], slots, count)
+
+    def second_field():
+        fill_columns(cols_c, own_c, halo.at[1], halo.at[3], slots, count)
 
     def step(q, _):
         outs = conv_step(cols_f, wide2, q, count)
@@ -264,7 +286,21 @@
             gfeat[:, 2 * q + par] = (grads[par] * gate).astype(BF16).reshape(count, 64, 128)
         return 0
 
-    lax.fori_loop(0, 4, step, 0)
+    bits = len(steps) // 2
+    work = {
+        0: weights,
+        1: first_field,
+        2: second_field,
+        bits - 1: lambda: lax.fori_loop(0, 2, step, 0),
+        2 * bits - 2: lambda: lax.fori_loop(2, 4, step, 0),
+    }
+    for n, (start, finish) in enumerate(steps):
+        if n:
+            start()
+        if n in work:
+            work[n]()
+        finish()
+    summed[...] = result[...]
 
 
 def shards(features, cotangent, weight_one, weight_two, occupancy, neighbours):
@@ -283,11 +319,8 @@
     slots = jnp.where(links >= 0, links - base[None], count).astype(jnp.int32)
 
     def swap(first, second, gate):
-        lows = [first[:, 0], second[:, 0]]
-        highs = [first[:, 7], second[:, 7]]
-        if gate is not None:
-            lows = [v * gate[:, 0] for v in lows]
-            highs = [v * gate[:, 7] for v in highs]
+        lows = [first[:, 0] * gate[:, 0], second[:, 0] * gate[:, 0]]
+        highs = [first[:, 7] * gate[:, 7], second[:, 7] * gate[:, 7]]
         before = lax.ppermute(jnp.stack(highs), "blocks", ups)
         after = lax.ppermute(jnp.stack(lows), "blocks", downs)
         return before[0], before[1], after[0], after[1]
@@ -317,29 +350,25 @@
     pieces = (3, peers, chunk, 128)
     bridge = [pltpu.VMEM(pieces, F32)] + [pltpu.VMEM(pieces, BF16)] * 3
     bridge += [pltpu.SemaphoreType.DMA((3, bits))] * 4
-    summed = pl.pallas_call(
-        functools.partial(sum_kernel, peers),
-        out_shape=jax.ShapeDtypeStruct(pieces, BF16),
-        in_specs=[vmem],
-        out_specs=vmem,
-        scratch_shapes=bridge,
+    out, gfeat, summed = pl.pallas_call(
+        functools.partial(back_kernel, peers, count),
+        out_shape=(field, field, jax.ShapeDtypeStruct(pieces, BF16)),
+        in_specs=[smem] + [vmem] * 6,
+        out_specs=(vmem,) * 3,
+        scratch_shapes=padded[:2]
+        + [pltpu.VMEM((4, count + 1, 64, 128), BF16)] * 2
+        + cols
+        + wides
+        + bridge[:4]
+        + [pltpu.SemaphoreType.DMA((2,))] * 2
+        + bridge[4:],
         compiler_params=pltpu.CompilerParams(
             vmem_limit_bytes=58 * 1024 * 1024, collective_id=0, has_side_effects=True
         ),
-        name="total",
-    )(grads.reshape(pieces))
+        name="back",
+    )(slots, act, gpre, mask, weight_one, weight_two, grads.reshape(pieces))
     summed = summed.reshape(3, chunk * peers, 128)[:, :2304].reshape(54, 128, 128).astype(F32)
     grad_one, grad_two = summed[:27], summed[27:]
-    out, gfeat = pl.pallas_call(
-        functools.partial(back_kernel, count),
-        out_shape=(field, field),
-        in_specs=[smem] + [vmem] * 9,
-        out_specs=(vmem,) * 2,
-        scratch_shapes=padded + cols + wides,
-        compiler_params=params,
-        cost_estimate=pl.CostEstimate(flops=6 * 10**9, bytes_accessed=10**7, transcendentals=0),
-        name="back",
-    )(slots, act, gpre, mask, *swap(act, gpre, None), weight_one, weight_two)
     return (
         out.reshape(features.shape),
         gfeat.reshape(features.shape),

time: 122 us -> 103 us (0.84)
  the two profiles are of different devices: /device:TPU:7 before, /device:TPU:0 now
where the time goes in v2:
time: 103 us
  Pallas kernels  84.4 us (82%)
  local copies, waits for them, and re-layouts  9.77 us (9%)
  starting transfers between devices  3.66 us (4%)
  other arithmetic  2.67 us (3%)
  waiting for transfers between devices  1.89 us (2%)
    pallas_call x1, Pallas kernels, shards(): pl.pallas_call(functools.partial(back_kernel, peers, count), out_shape=(f...  58.7 us
    pallas_call x1, Pallas kernels, shards(): pl.pallas_call(functools.partial(front_kernel, count), out_shape=(field,...  25.6 us
    ppermute x1, starting transfers between devices, swap(): before = lax.ppermute(jnp.stack(highs), 'blocks', ups)  2.37 us
    unnamed x7, local copies, waits for them, and re-layouts  2.3 us
    slice x1, local copies, waits for them, and re-layouts, shards(): grad_one, grad_two = (summed[:27], summed[27:])  2.21 us
  transfers between devices with their start and end apart: 2, of which 1 were waited for; matrix products, arithmetic and copies ran while one was open for 2% of the time, Pallas kernels for 0%

profile of v2, /device:TPU:0, one launch (start us, length us, event | category | flops | bytes accessed | tf_op | source)
XLA Modules:
  0.0 103.1 jit_solution(16886622185618635233)
XLA Ops:
  0.6 0.7 convert_element_type.9
  1.4 0.1 broadcast_in_dim.22
  1.5 1.2 %fusion = (bf16[1,6,64,128]{3,2,1,0:T(8,128)(2,1)S(1)}, bf16[1,6,64,128]{3,2,1,0:T(8,128)(2,1)S(1)}, bf16[1,6,64,128]{3,2,1,0:T(8,128)(2,1)S(1)}, bf16[1,6,64,128]{3,2,1,0:T(8,128)(2,1)S(1)}) fusion(bf16[6,8,64,128]{3,2,1,0:T(8,128)(2,1)} %bitcast.51, bf16[6,64]{1,0:T(8,128)(2,1)S(1)} %get-tuple-element.32, bf16[6,64]{1,0:T(8,128)(2,1)S(1)} %get-tuple-element.33, ...), kind=kLoop, calls=%fused_computation.5 | loop fusion | flops 196608 | bytes 787968 | tf_op jit(solution)/shard_map/mul | solution.py:322
  2.7 2.4 %collective-permute-start = (bf16[2,6,64,128]{3,2,1,0:T(8,128)(2,1)S(1)}, bf16[2,6,64,128]{3,2,1,0:T(8,128)(2,1)S(1)}, u32[]{:S(2)}, u32[]{:S(2)}) collective-permute-start(bf16[2,6,64,128]{3,2,1,0:T(8,128)(2,1)S(1)} %pad_maximum_fusion), channel_id=1, source_target_pairs={{0,1},{1,2},{2,3},{3,4},{4,5},{5,6},{6,7},{7,8},{8,9},{9,10},{10,1... | collective-permute-start | bytes 589832 | tf_op jit(solution)/shard_map/ppermute | solution.py:324
  5.1 1.3 %collective-permute-start.1 = (bf16[2,6,64,128]{3,2,1,0:T(8,128)(2,1)S(1)}, bf16[2,6,64,128]{3,2,1,0:T(8,128)(2,1)S(1)}, u32[]{:S(2)}, u32[]{:S(2)}) collective-permute-start(bf16[2,6,64,128]{3,2,1,0:T(8,128)(2,1)S(1)} %pad_maximum_fusion.1), channel_id=1, source_target_pairs={{1,0},{2,1},{3,2},{4,3},{5,4},{6,5},{7,6},{8,7},{9,8},{10,9},{11,1... | collective-permute-start | bytes 589832 | tf_op jit(solution)/shard_map/ppermute | solution.py:325
  6.5 0.8 fusion.9
  7.3 0.7 subtract_select_fusion.slots
  8.0 0.0 collective-permute-done
  8.0 0.7 slice_bitcast_fusion.4
  8.7 1.9 %collective-permute-done.1 = bf16[2,6,64,128]{3,2,1,0:T(8,128)(2,1)S(1)} collective-permute-done((bf16[2,6,64,128]{3,2,1,0:T(8,128)(2,1)S(1)}, bf16[2,6,64,128]{3,2,1,0:T(8,128)(2,1)S(1)}, u32[]{:S(2)}, u32[]{:S(2)}) %collective-permute-start.1) | collective-permute-done | bytes 196640 | tf_op jit(solution)/shard_map/ppermute | solution.py:325
  10.6 0.7 slice_bitcast_fusion
  11.2 1.4 %broadcast_in_dim.23.mask = bf16[6,8,64,128]{3,2,1,0:T(8,128)(2,1)} broadcast(bf16[6,8,64]{2,1,0:T(8,128)(2,1)S(1)} %broadcast_in_dim.22), dimensions={0,1,2} | broadcast | bytes 792576 | tf_op jit(solution)/shard_map/broadcast_in_dim | solution.py:313
  12.6 25.6 %front.1 = (bf16[6,8,64,128]{3,2,1,0:T(8,128)(2,1)}, bf16[6,8,64,128]{3,2,1,0:T(8,128)(2,1)}, f32[3,2560,128]{2,1,0:T(8,128)}) custom-call(s32[6,27]{1,0:T(8,128)} %subtract_select_fusion.slots, bf16[6,8,64,128]{3,2,1,0:T(8,128)(2,1)} %bitcast.50, bf16[6,8,64,128]{3,2,1,0:T(8,128)(2,1)} %bitcast.52, bf16[6,8,64,128]{3,2,1,0:T(8,128)(2,1)} %broadcast_in_dim.23.mask, ...), custom_call_target="tpu_custom_call" | custom-call | flops 11000000512 | bytes 10000000 | tf_op jit(solution)/shard_map/front/pallas_call | solution.py:340
  38.2 58.7 %back.1 = (bf16[6,8,64,128]{3,2,1,0:T(8,128)(2,1)}, bf16[6,8,64,128]{3,2,1,0:T(8,128)(2,1)}, bf16[3,32,80,128]{3,2,1,0:T(8,128)(2,1)}) custom-call(s32[6,27]{1,0:T(8,128)} %subtract_select_fusion.slots, bf16[6,8,64,128]{3,2,1,0:T(8,128)(2,1)} %get-tuple-element.10.act, bf16[6,8,64,128]{3,2,1,0:T(8,128)(2,1)} %get-tuple-element.11.gpre, ...), custom_call_target="tpu_custom_call" | custom-call | tf_op jit(solution)/shard_map/back/pallas_call | solution.py:353
  96.9 1.6 %slice.74 = bf16[3,2304,128]{2,1,0:T(8,128)(2,1)S(1)} slice(bf16[3,2560,128]{2,1,0:T(8,128)(2,1)} %bitcast.46), slice={[0:3], [0:2304], [0:128]} | slice | bytes 3538944 | tf_op jit(solution)/shard_map/slice | solution.py:370
  98.5 0.0 copy-start.1
  98.6 2.2 %fusion.7 = (f32[27,128,128]{2,1,0:T(8,128)}, f32[27,128,128]{2,1,0:T(8,128)}) fusion(bf16[54,128,128]{2,1,0:T(8,128)(2,1)S(1)} %bitcast.44), kind=kLoop, calls=%fused_computation.26 | loop fusion | bytes 7077888 | tf_op jit(solution)/shard_map/slice | solution.py:371
  100.8 0.0 copy-start
  100.8 0.0 copy-done.1
  100.8 0.9 copy.31
  101.7 0.5 copy-done
  102.2 0.9 copy.32
  (6 shorter events, 0.1 us)
Async XLA Ops:
  2.7 5.3 %collective-permute-start = (bf16[2,6,64,128]{3,2,1,0:T(8,128)(2,1)S(1)}, bf16[2,6,64,128]{3,2,1,0:T(8,128)(2,1)S(1)}, u32[]{:S(2)}, u32[]{:S(2)}) collective-permute-start(bf16[2,6,64,128]{3,2,1,0:T(8,128)(2,1)S(1)} %pad_maximum_fusion), channel_id=1, source_target_pairs={{0,1},{1,2},{2,3},{3,4},{4,5},{5,6},{6,7},{7,8},{8,9},{9,10},{10,1... | collective-permute-start | bytes 589832 | tf_op jit(solution)/shard_map/ppermute | solution.py:324
  5.1 5.4 %collective-permute-start.1 = (bf16[2,6,64,128]{3,2,1,0:T(8,128)(2,1)S(1)}, bf16[2,6,64,128]{3,2,1,0:T(8,128)(2,1)S(1)}, u32[]{:S(2)}, u32[]{:S(2)}) collective-permute-start(bf16[2,6,64,128]{3,2,1,0:T(8,128)(2,1)S(1)} %pad_maximum_fusion.1), channel_id=1, source_target_pairs={{1,0},{2,1},{3,2},{4,3},{5,4},{6,5},{7,6},{8,7},{9,8},{10,9},{11,1... | collective-permute-start | bytes 589832 | tf_op jit(solution)/shard_map/ppermute | solution.py:325
  98.5 2.2 %copy-start.1 = (bf16[6,8,64,128]{3,2,1,0:T(8,128)(2,1)S(1)}, bf16[6,8,64,128]{3,2,1,0:T(8,128)(2,1)}, u32[]{:S(2)}) copy-start(bf16[6,8,64,128]{3,2,1,0:T(8,128)(2,1)} %get-tuple-element.13) | copy-start | bytes 2359300
  100.8 1.4 %copy-start = (bf16[6,8,64,128]{3,2,1,0:T(8,128)(2,1)S(1)}, bf16[6,8,64,128]{3,2,1,0:T(8,128)(2,1)}, u32[]{:S(2)}) copy-start(bf16[6,8,64,128]{3,2,1,0:T(8,128)(2,1)} %get-tuple-element.14) | copy-start | bytes 2359300

commit v3 on v2

--- a/solution.py
+++ b/solution.py
@@ -185,32 +185,28 @@
             device_id_type=pl.DeviceIdType.MESH,
         )
 
-    def start_halve(s):
+    def start_halve(s, part):
         source = grads if s == 0 else total
-        for part in range(3):
-            other, half, _, copy = halve(part, s)
-            outbox[part, pl.ds(other, half)] = source[part, pl.ds(other, half)].astype(BF16)
-            copy.start()
-
-    def finish_halve(s):
+        other, half, _, copy = halve(part, s)
+        outbox[part, pl.ds(other, half)] = source[part, pl.ds(other, half)].astype(BF16)
+        copy.start()
+
+    def finish_halve(s, part):
         source = grads if s == 0 else total
-        for part in range(3):
-            _, half, at, copy = halve(part, s)
-            copy.wait()
-            mine = pl.ds(lows[part][s + 1], half)
-            value = source[part, mine] + inbox[part, at : at + half].astype(F32)
-            if s == bits - 1:
-                result[part, mine] = value.astype(BF16)
-            else:
-                total[part, mine] = value
-
-    def start_double(s):
-        for part in range(3):
-            double(part, s).start()
-
-    def finish_double(s):
-        for part in range(3):
-            double(part, s).wait()
+        _, half, at, copy = halve(part, s)
+        copy.wait()
+        mine = pl.ds(lows[part][s + 1], half)
+        value = source[part, mine] + inbox[part, at : at + half].astype(F32)
+        if s == bits - 1:
+            result[part, mine] = value.astype(BF16)
+        else:
+            total[part, mine] = value
+
+    def start_double(s, part):
+        double(part, s).start()
+
+    def finish_double(s, part):
+        double(part, s).wait()
 
     steps = [(functools.partial(start_halve, s), functools.partial(finish_halve, s)) for s in range(bits)]
     steps += [
@@ -242,7 +238,8 @@
     me = lax.axis_index("blocks")
     rows = count * 64
     steps = sum_steps(peers, grads, total, outbox, inbox, result, sems)
-    steps[0][0]()
+    for part in range(3):
+        steps[0][0](part)
 
     for i, (field, x) in enumerate(((act, 7), (gpre, 7), (act, 0), (gpre, 0))):
         edges[i, :count] = field[:, x]
@@ -294,13 +291,15 @@
         bits - 1: lambda: lax.fori_loop(0, 2, step, 0),
         2 * bits - 2: lambda: lax.fori_loop(2, 4, step, 0),
     }
-    for n, (start, finish) in enumerate(steps):
-        if n:
-            start()
+    for n, (_, finish) in enumerate(steps):
         if n in work:
             work[n]()
-        finish()
-    summed[...] = result[...]
+        for part in range(3):
+            finish(part)
+            if n + 1 < len(steps):
+                steps[n + 1][0](part)
+            else:
+                summed[part] = result[part]
 
 
 def shards(features, cotangent, weight_one, weight_two, occupancy, neighbours):

time: 103 us -> 102 us (level)
  Pallas kernels: 84.4 us -> 82.5 us
    pallas_call x1, Pallas kernels: 58.7 us -> 56.8 us  [shards(): pl.pallas_call(functools.partial(back_kernel, peers, count), out_shape=(f...]
where the time goes in v3:
time: 102 us; the launch traced here: 101 us
  Pallas kernels  82.5 us (81%)
  local copies, waits for them, and re-layouts  9.77 us (10%)
  starting transfers between devices  3.66 us (4%)
  other arithmetic  2.67 us (3%)
  waiting for transfers between devices  1.89 us (2%)
    pallas_call x1, Pallas kernels, shards(): pl.pallas_call(functools.partial(back_kernel, peers, count), out_shape=(f...  56.8 us
    pallas_call x1, Pallas kernels, shards(): pl.pallas_call(functools.partial(front_kernel, count), out_shape=(field,...  25.6 us
    ppermute x1, starting transfers between devices, swap(): before = lax.ppermute(jnp.stack(highs), 'blocks', ups)  2.37 us
    unnamed x7, local copies, waits for them, and re-layouts  2.3 us
    slice x1, local copies, waits for them, and re-layouts, shards(): grad_one, grad_two = (summed[:27], summed[27:])  2.21 us
  transfers between devices with their start and end apart: 2, of which 1 were waited for; matrix products, arithmetic and copies ran while one was open for 2% of the time, Pallas kernels for 0%

profile of v3, /device:TPU:0, one launch (start us, length us, event | category | flops | bytes accessed | tf_op | source)
XLA Modules:
  0.0 101.2 jit_solution(10583376724267458299)
XLA Ops:
  0.6 0.7 convert_element_type.9
  1.4 0.1 broadcast_in_dim.22
  1.5 1.2 %fusion = (bf16[1,6,64,128]{3,2,1,0:T(8,128)(2,1)S(1)}, bf16[1,6,64,128]{3,2,1,0:T(8,128)(2,1)S(1)}, bf16[1,6,64,128]{3,2,1,0:T(8,128)(2,1)S(1)}, bf16[1,6,64,128]{3,2,1,0:T(8,128)(2,1)S(1)}) fusion(bf16[6,8,64,128]{3,2,1,0:T(8,128)(2,1)} %bitcast.51, bf16[6,64]{1,0:T(8,128)(2,1)S(1)} %get-tuple-element.32, bf16[6,64]{1,0:T(8,128)(2,1)S(1)} %get-tuple-element.33, ...), kind=kLoop, calls=%fused_computation.5 | loop fusion | flops 196608 | bytes 787968 | tf_op jit(solution)/shard_map/mul | solution.py:321
  2.7 2.4 %collective-permute-start = (bf16[2,6,64,128]{3,2,1,0:T(8,128)(2,1)S(1)}, bf16[2,6,64,128]{3,2,1,0:T(8,128)(2,1)S(1)}, u32[]{:S(2)}, u32[]{:S(2)}) collective-permute-start(bf16[2,6,64,128]{3,2,1,0:T(8,128)(2,1)S(1)} %pad_maximum_fusion), channel_id=1, source_target_pairs={{0,1},{1,2},{2,3},{3,4},{4,5},{5,6},{6,7},{7,8},{8,9},{9,10},{10,1... | collective-permute-start | bytes 589832 | tf_op jit(solution)/shard_map/ppermute | solution.py:323
  5.1 1.3 %collective-permute-start.1 = (bf16[2,6,64,128]{3,2,1,0:T(8,128)(2,1)S(1)}, bf16[2,6,64,128]{3,2,1,0:T(8,128)(2,1)S(1)}, u32[]{:S(2)}, u32[]{:S(2)}) collective-permute-start(bf16[2,6,64,128]{3,2,1,0:T(8,128)(2,1)S(1)} %pad_maximum_fusion.1), channel_id=1, source_target_pairs={{1,0},{2,1},{3,2},{4,3},{5,4},{6,5},{7,6},{8,7},{9,8},{10,9},{11,1... | collective-permute-start | bytes 589832 | tf_op jit(solution)/shard_map/ppermute | solution.py:324
  6.5 0.8 fusion.9
  7.3 0.7 subtract_select_fusion.slots
  8.0 0.0 collective-permute-done
  8.0 0.7 slice_bitcast_fusion.4
  8.7 1.9 %collective-permute-done.1 = bf16[2,6,64,128]{3,2,1,0:T(8,128)(2,1)S(1)} collective-permute-done((bf16[2,6,64,128]{3,2,1,0:T(8,128)(2,1)S(1)}, bf16[2,6,64,128]{3,2,1,0:T(8,128)(2,1)S(1)}, u32[]{:S(2)}, u32[]{:S(2)}) %collective-permute-start.1) | collective-permute-done | bytes 196640 | tf_op jit(solution)/shard_map/ppermute | solution.py:324
  10.6 0.7 slice_bitcast_fusion
  11.2 1.4 %broadcast_in_dim.23.mask = bf16[6,8,64,128]{3,2,1,0:T(8,128)(2,1)} broadcast(bf16[6,8,64]{2,1,0:T(8,128)(2,1)S(1)} %broadcast_in_dim.22), dimensions={0,1,2} | broadcast | bytes 792576 | tf_op jit(solution)/shard_map/broadcast_in_dim | solution.py:312
  12.6 25.6 %front.1 = (bf16[6,8,64,128]{3,2,1,0:T(8,128)(2,1)}, bf16[6,8,64,128]{3,2,1,0:T(8,128)(2,1)}, f32[3,2560,128]{2,1,0:T(8,128)}) custom-call(s32[6,27]{1,0:T(8,128)} %subtract_select_fusion.slots, bf16[6,8,64,128]{3,2,1,0:T(8,128)(2,1)} %bitcast.50, bf16[6,8,64,128]{3,2,1,0:T(8,128)(2,1)} %bitcast.52, bf16[6,8,64,128]{3,2,1,0:T(8,128)(2,1)} %broadcast_in_dim.23.mask, ...), custom_call_target="tpu_custom_call" | custom-call | flops 11000000512 | bytes 10000000 | tf_op jit(solution)/shard_map/front/pallas_call | solution.py:339
  38.2 56.8 %back.1 = (bf16[6,8,64,128]{3,2,1,0:T(8,128)(2,1)}, bf16[6,8,64,128]{3,2,1,0:T(8,128)(2,1)}, bf16[3,32,80,128]{3,2,1,0:T(8,128)(2,1)}) custom-call(s32[6,27]{1,0:T(8,128)} %subtract_select_fusion.slots, bf16[6,8,64,128]{3,2,1,0:T(8,128)(2,1)} %get-tuple-element.10.act, bf16[6,8,64,128]{3,2,1,0:T(8,128)(2,1)} %get-tuple-element.11.gpre, ...), custom_call_target="tpu_custom_call" | custom-call | tf_op jit(solution)/shard_map/back/pallas_call | solution.py:352
  95.1 1.6 %slice.74 = bf16[3,2304,128]{2,1,0:T(8,128)(2,1)S(1)} slice(bf16[3,2560,128]{2,1,0:T(8,128)(2,1)} %bitcast.46), slice={[0:3], [0:2304], [0:128]} | slice | bytes 3538944 | tf_op jit(solution)/shard_map/slice | solution.py:369
  96.7 0.0 copy-start.1
  96.7 2.2 %fusion.7 = (f32[27,128,128]{2,1,0:T(8,128)}, f32[27,128,128]{2,1,0:T(8,128)}) fusion(bf16[54,128,128]{2,1,0:T(8,128)(2,1)S(1)} %bitcast.44), kind=kLoop, calls=%fused_computation.26 | loop fusion | bytes 7077888 | tf_op jit(solution)/shard_map/slice | solution.py:370
  98.9 0.0 copy-start
  98.9 0.0 copy-done.1
  98.9 0.9 copy.31
  99.8 0.5 copy-done
  100.3 0.9 copy.32
  (6 shorter events, 0.1 us)
Async XLA Ops:
  2.7 5.3 %collective-permute-start = (bf16[2,6,64,128]{3,2,1,0:T(8,128)(2,1)S(1)}, bf16[2,6,64,128]{3,2,1,0:T(8,128)(2,1)S(1)}, u32[]{:S(2)}, u32[]{:S(2)}) collective-permute-start(bf16[2,6,64,128]{3,2,1,0:T(8,128)(2,1)S(1)} %pad_maximum_fusion), channel_id=1, source_target_pairs={{0,1},{1,2},{2,3},{3,4},{4,5},{5,6},{6,7},{7,8},{8,9},{9,10},{10,1... | collective-permute-start | bytes 589832 | tf_op jit(solution)/shard_map/ppermute | solution.py:323
  5.1 5.4 %collective-permute-start.1 = (bf16[2,6,64,128]{3,2,1,0:T(8,128)(2,1)S(1)}, bf16[2,6,64,128]{3,2,1,0:T(8,128)(2,1)S(1)}, u32[]{:S(2)}, u32[]{:S(2)}) collective-permute-start(bf16[2,6,64,128]{3,2,1,0:T(8,128)(2,1)S(1)} %pad_maximum_fusion.1), channel_id=1, source_target_pairs={{1,0},{2,1},{3,2},{4,3},{5,4},{6,5},{7,6},{8,7},{9,8},{10,9},{11,1... | collective-permute-start | bytes 589832 | tf_op jit(solution)/shard_map/ppermute | solution.py:324
  96.7 2.2 %copy-start.1 = (bf16[6,8,64,128]{3,2,1,0:T(8,128)(2,1)S(1)}, bf16[6,8,64,128]{3,2,1,0:T(8,128)(2,1)}, u32[]{:S(2)}) copy-start(bf16[6,8,64,128]{3,2,1,0:T(8,128)(2,1)} %get-tuple-element.13) | copy-start | bytes 2359300
  98.9 1.4 %copy-start = (bf16[6,8,64,128]{3,2,1,0:T(8,128)(2,1)S(1)}, bf16[6,8,64,128]{3,2,1,0:T(8,128)(2,1)}, u32[]{:S(2)}) copy-start(bf16[6,8,64,128]{3,2,1,0:T(8,128)(2,1)} %get-tuple-element.14) | copy-start | bytes 2359300
